TPU v7x, 32 devices: a whole 2x2x4 slice. The times are simulated.
32 devices in a mesh: parts: 2 (over y), tm: 4 (over z), tile: 2 (over x), chan: 2 (over core).
Axes of the slice: x: 2, y: 2, z: 4, core: 2. Of those that a mesh axis runs over, the one named last changes fastest.
Arguments:
- pillar_feat: bfloat16 [128, 192, 128], P(('parts', 'tm'), 'tile'), parts along dimension 0, may hold values from -6 to 6
- pillar_cell: int32 [128, 192], P(('parts', 'tm'), 'tile'), parts along dimension 0, may hold values from 0 to 191
- pillar_count: int32 [128, 192], P(('parts', 'tm'), 'tile'), parts along dimension 0, may hold values from 1 to 32
- sweep_embed: bfloat16 [128, 128], P(('parts', 'tm')), parts along dimension 0, may hold values from -3 to 3
- conv_weight: bfloat16 [9, 128, 256], P(None, None, 'chan'), may hold values from -0.5 to 0.5
- proj_weight: bfloat16 [3, 2, 128, 128], P(None, 'chan'), may hold values from -0.5 to 0.5
- d_out: bfloat16 [128, 384, 256], P(('parts', 'tm'), 'tile', 'chan'), parts along dimension 0, may hold values from -0.0390625 to 0.0390625
Outputs:
- attn_out: bfloat16 [128, 384, 256], P(('parts', 'tm'), 'tile', 'chan'), parts along dimension 0
- grad_conv: float32 [9, 256, 256], P(None, 'parts', 'chan'), parts along dimension 1
- grad_proj: float32 [3, 2, 256, 128], P(None, 'chan', 'parts'), parts along dimension 2
There are 2 independent parts, one for each index of `parts`. A program takes and returns all parts, laid end to end along the dimension named above; an argument that names none is the same for every part. Nothing has to cross between parts.
Inputs may be any that keep to these rules, and one draw needn't show every extreme that they name: `pillar_cell`: the cell within the tile's 3 rows of 64 cells, row-major.
All inputs are finite; a program needn't handle non-finite values.
Results may differ from a plain program's by a relative error of at most 0.0069.
Values may be sent and summed in bfloat16 or wider, within the bound.
A program may use at most 64 MiB of HBM per device.

v0:
```python
import jax
import jax.numpy as jnp
from jax import lax
from jax.sharding import PartitionSpec as P

TH = 3
W = 64


def prefix(value, axis, combine, identity, reverse):
    count, here = (lax.axis_size(axis), lax.axis_index(axis))
    everything = lax.all_gather(value, axis)
    start = jnp.broadcast_to(jnp.asarray(identity, value.dtype), value.shape)

    def hop(k, before):
        at = count - 1 - k if reverse else k
        reached = at > here if reverse else at < here
        new = combine(before, everything[at])
        return jnp.where(reached, new, before)

    return lax.fori_loop(0, count, hop, start)


def add_one(earlier, later):
    return earlier + later


def reverse_cumsum(array_in):
    return jnp.flip(jnp.cumsum(jnp.flip(array_in, 0), 0), 0)


def boundary_whole(total_kv, total_cot):
    zeros_like = jnp.zeros_like(total_kv)
    before = prefix(total_kv, ("tm", "tile"), add_one, zeros_like, False)
    after = prefix(total_cot, ("tm", "tile"), add_one, zeros_like, True)
    return (before, after)


def make_grid(pillar_feat, pillar_cell, pillar_count, embed, groups):
    sweep_count, pillar_all, channels = pillar_feat.shape
    per_group = pillar_all // groups
    cell_count = TH * W
    counts_f = pillar_count.astype(jnp.float32)
    count_gate = counts_f / (counts_f + 8.0)
    weighted = (pillar_feat.astype(jnp.float32) * count_gate[:, :, None]).reshape(
        sweep_count, groups, per_group, channels
    )
    cells = pillar_cell.reshape(sweep_count, groups, per_group)
    onehot = (
        cells[:, :, :, None] == jnp.arange(cell_count, dtype=jnp.int32)[None, None, None, :]
    ).astype(jnp.float32)
    scattered = jnp.einsum("tgpn,tgpc->tgnc", onehot, weighted, precision=lax.Precision.HIGHEST)
    bev_grid = (scattered + embed.astype(jnp.float32)[:, None, None, :]).astype(jnp.bfloat16)
    return bev_grid.reshape(sweep_count, groups * TH, W, channels)


def forward_local(padded_rows, conv_weight, proj_weight):
    sweep_count = padded_rows.shape[0]
    row_count = padded_rows.shape[1] - 2
    col_count = padded_rows.shape[2]
    head_count = proj_weight.shape[1]
    head_size = proj_weight.shape[2]
    width_out = head_count * head_size
    padded = jnp.pad(padded_rows, ((0, 0), (0, 0), (1, 1), (0, 0)))
    shifted_list = []
    for offset in range(9):
        row_off = offset // 3
        col_off = offset % 3
        shifted_list.append(
            padded[:, row_off : row_off + row_count, col_off : col_off + col_count, :]
        )
    preact = jnp.zeros((sweep_count, row_count, col_count, width_out), jnp.float32)
    for offset in range(9):
        preact = preact + jnp.einsum(
            "tywc,cj->tywj",
            shifted_list[offset],
            conv_weight[offset],
            preferred_element_type=jnp.float32,
        )
    features = (
        jax.nn.silu(preact)
        .astype(jnp.bfloat16)
        .reshape(sweep_count, row_count * col_count, head_count, head_size)
    )
    query = jnp.einsum(
        "tnhc,hcd->tnhd", features, proj_weight[0], preferred_element_type=jnp.float32
    ).astype(jnp.bfloat16)
    keys = jnp.einsum(
        "tnhc,hcd->tnhd", features, proj_weight[1], preferred_element_type=jnp.float32
    ).astype(jnp.bfloat16)
    values = jnp.einsum(
        "tnhc,hcd->tnhd", features, proj_weight[2], preferred_element_type=jnp.float32
    ).astype(jnp.bfloat16)
    return (shifted_list, preact, features, query, keys, values)


def backward_local(
    shifted_list,
    preact,
    features,
    query,
    keys,
    values,
    scaled_cot,
    scale,
    kv_state,
    adjoint,
    proj_weight,
):
    highest = lax.Precision.HIGHEST
    query_f = query.astype(jnp.float32)
    attn_out = (
        jnp.einsum("tnhc,thcd->tnhd", query_f, kv_state, precision=highest)
        * scale[:, None, None, None]
    ).astype(jnp.bfloat16)
    grad_query = jnp.einsum(
        "tnhd,thcd->tnhc", scaled_cot.astype(jnp.float32), kv_state, precision=highest
    ).astype(jnp.bfloat16)
    grad_keys = jnp.einsum(
        "tnhd,thcd->tnhc", values.astype(jnp.float32), adjoint, precision=highest
    ).astype(jnp.bfloat16)
    grad_values = jnp.einsum(
        "tnhc,thcd->tnhd", keys.astype(jnp.float32), adjoint, precision=highest
    ).astype(jnp.bfloat16)
    grad_proj = jnp.stack(
        [
            jnp.einsum("tnhc,tnhd->hcd", features, grad_query, preferred_element_type=jnp.float32),
            jnp.einsum("tnhc,tnhd->hcd", features, grad_keys, preferred_element_type=jnp.float32),
            jnp.einsum("tnhc,tnhd->hcd", features, grad_values, preferred_element_type=jnp.float32),
        ],
        0,
    )
    grad_feat = jnp.einsum(
        "tnhd,hcd->tnhc", grad_query, proj_weight[0], preferred_element_type=jnp.float32
    )
    grad_feat = grad_feat + jnp.einsum(
        "tnhd,hcd->tnhc", grad_keys, proj_weight[1], preferred_element_type=jnp.float32
    )
    grad_feat = grad_feat + jnp.einsum(
        "tnhd,hcd->tnhc", grad_values, proj_weight[2], preferred_element_type=jnp.float32
    )
    logistic = jax.nn.sigmoid(preact)
    grad_pre = (
        grad_feat.reshape(preact.shape) * logistic * (1.0 + preact * (1.0 - logistic))
    ).astype(jnp.bfloat16)
    grad_list = []
    for offset in range(9):
        grad_list.append(
            jnp.einsum(
                "tywc,tywj->cj", shifted_list[offset], grad_pre, preferred_element_type=jnp.float32
            )
        )
    grad_conv = jnp.stack(grad_list, 0)
    sweep_count = attn_out.shape[0]
    return (attn_out.reshape(sweep_count, attn_out.shape[1], -1), grad_conv, grad_proj)


def local(pillar_feat, pillar_cell, pillar_count, sweep_embed, conv_weight, proj_weight, d_out):
    sweep_block = pillar_feat.shape[0]
    head_count = proj_weight.shape[1]
    head_size = proj_weight.shape[2]
    tile_count = lax.axis_size("tile")
    total_cells = TH * W * tile_count
    feat_all, cell_all, count_all, cot_in = (
        lax.all_to_all(pillar_feat, "tile", split_axis=0, concat_axis=1, tiled=True),
        lax.all_to_all(pillar_cell, "tile", split_axis=0, concat_axis=1, tiled=True),
        lax.all_to_all(pillar_count, "tile", split_axis=0, concat_axis=1, tiled=True),
        lax.all_to_all(d_out, "tile", split_axis=0, concat_axis=1, tiled=True),
    )
    sweep_count = feat_all.shape[0]
    tile_index = lax.axis_index("tile")
    embed = lax.dynamic_slice_in_dim(sweep_embed, tile_index * sweep_count, sweep_count, 0)
    bev_grid = make_grid(feat_all, cell_all, count_all, embed, tile_count)
    padded_rows = jnp.pad(bev_grid, ((0, 0), (1, 1), (0, 0), (0, 0)))
    shifted_list, preact, features, query, keys, values = forward_local(
        padded_rows, conv_weight, proj_weight
    )
    sweep_index = (
        lax.axis_index("tm") * sweep_block
        + tile_index * sweep_count
        + jnp.arange(sweep_count, dtype=jnp.int32)
    )
    scale = 1.0 / ((sweep_index + 1).astype(jnp.float32) * jnp.float32(total_cells))
    scaled_cot = (
        cot_in.astype(jnp.float32).reshape(sweep_count, total_cells, head_count, head_size)
        * scale[:, None, None, None]
    ).astype(jnp.bfloat16)
    pair_local = jnp.einsum("tnhc,tnhd->thcd", keys, values, preferred_element_type=jnp.float32)
    cot_local = jnp.einsum("tnhc,tnhd->thcd", query, scaled_cot, preferred_element_type=jnp.float32)
    before, after = boundary_whole(jnp.sum(pair_local, 0), jnp.sum(cot_local, 0))
    kv_state = before[None] + jnp.cumsum(pair_local, 0)
    adjoint = after[None] + reverse_cumsum(cot_local)
    whole_out, grad_conv, grad_proj = backward_local(
        shifted_list,
        preact,
        features,
        query,
        keys,
        values,
        scaled_cot,
        scale,
        kv_state,
        adjoint,
        proj_weight,
    )
    attn_out = lax.all_to_all(whole_out, "tile", split_axis=1, concat_axis=0, tiled=True)
    grad_conv, grad_proj = lax.psum((grad_conv, grad_proj), ("tm", "tile"))
    return (attn_out, grad_conv, grad_proj)


def solution(mesh):
    return jax.shard_map(
        local,
        mesh=mesh,
        in_specs=(
            P(("parts", "tm"), "tile", None),
            P(("parts", "tm"), "tile"),
            P(("parts", "tm"), "tile"),
            P(("parts", "tm"), None),
            P(None, None, "chan"),
            P(None, "chan", None, None),
            P(("parts", "tm"), "tile", "chan"),
        ),
        out_specs=(
            P(("parts", "tm"), "tile", "chan"),
            P(None, "parts", "chan"),
            P(None, "chan", "parts", None),
        ),
        check_vma=False,
    )
```

profile of v0, /device:TPU:0, one launch (start us, length us, event | category | flops | bytes accessed | tf_op | source)
XLA Modules:
  0.0 233.4 jit_solution(1407072980223376086)
XLA Ops:
  7.2 4.2 %all-to-all-start.2 = ((s32[2,8,96]{2,1,0:T(8,128)}), s32[2,8,96]{2,1,0:T(8,128)S(1)}, u32[]{:S(2)}, u32[]{:S(2)}) async-start(s32[2,8,96]{2,1,0:T(8,128)} %bitcast.321), calls=%async_computation.2 | async-start | bytes 16384 | tf_op jit(solution)/shard_map/all_to_all | solution.py:167
  11.4 0.7 dynamic-slice_convert_fusion
  12.1 3.1 %all-to-all-done.2 = s32[2,8,96]{2,1,0:T(8,128)S(1)} async-done(((s32[2,8,96]{2,1,0:T(8,128)}), s32[2,8,96]{2,1,0:T(8,128)S(1)}, u32[]{:S(2)}, u32[]{:S(2)}) %all-to-all-start.2) | async-done | bytes 6176 | tf_op jit(solution)/shard_map/all_to_all | solution.py:167
  15.2 3.2 %all-to-all-start = ((s32[2,8,96]{2,1,0:T(8,128)}), s32[2,8,96]{2,1,0:T(8,128)S(1)}, u32[]{:S(2)}, u32[]{:S(2)}) async-start(s32[2,8,96]{2,1,0:T(8,128)} %bitcast.322), calls=%async_computation | async-start | bytes 16384 | tf_op jit(solution)/shard_map/all_to_all | solution.py:166
  18.5 3.8 %all-to-all-done = s32[2,8,96]{2,1,0:T(8,128)S(1)} async-done(((s32[2,8,96]{2,1,0:T(8,128)}), s32[2,8,96]{2,1,0:T(8,128)S(1)}, u32[]{:S(2)}, u32[]{:S(2)}) %all-to-all-start) | async-done | bytes 6176 | tf_op jit(solution)/shard_map/all_to_all | solution.py:166
  22.2 3.5 %all-to-all-start.1 = ((bf16[16,96,128]{2,1,0:T(8,128)(2,1)}), bf16[16,96,128]{2,1,0:T(8,128)(2,1)S(1)}, u32[]{:S(2)}, u32[]{:S(2)}) async-start(bf16[16,96,128]{2,1,0:T(8,128)(2,1)} %param.11), calls=%async_computation.1 | async-start | bytes 786432 | tf_op jit(solution)/shard_map/all_to_all | solution.py:165
  25.8 5.8 %all-to-all-done.1 = bf16[16,96,128]{2,1,0:T(8,128)(2,1)S(1)} async-done(((bf16[16,96,128]{2,1,0:T(8,128)(2,1)}), bf16[16,96,128]{2,1,0:T(8,128)(2,1)S(1)}, u32[]{:S(2)}, u32[]{:S(2)}) %all-to-all-start.1) | async-done | bytes 393248 | tf_op jit(solution)/shard_map/all_to_all | solution.py:165
  31.6 3.5 %all-to-all-start.4 = ((bf16[16,192,128]{2,1,0:T(8,128)(2,1)}), bf16[16,192,128]{2,1,0:T(8,128)(2,1)S(1)}, u32[]{:S(2)}, u32[]{:S(2)}) async-start(bf16[16,192,128]{2,1,0:T(8,128)(2,1)} %param.17), calls=%async_computation.4 | async-start | bytes 1572864 | tf_op jit(solution)/shard_map/all_to_all | solution.py:168
  35.2 1.1 add_convert_fusion
  39.2 2.1 multiply_convert_fusion.1
  42.0 0.9 copy-done
  43.3 34.4 %all-gather = f32[1024,128]{1,0:T(8,128)} all-gather(f32[128,128]{1,0:T(8,128)S(1)} %get-tuple-element.244), channel_id=2, replica_groups=mesh['parts'=2,'tm'=4,'tile'=2,'chan'=2] {'tm','tile'}, dimensions={0}, use_global_device_ids=true | all-gather | bytes 589824 | tf_op jit(solution)/shard_map/all_gather | solution.py:12
  77.8 7.0 %while.30 = (s32[]{:T(128)}, f32[1,128,128]{2,1,0:T(8,128)S(1)}, s32[]{:T(128)}, f32[8,1,128,128]{3,2,1,0:T(8,128)}, s32[]{:T(128)}, /*index=5*/s32[]{:T(128)}) while((s32[]{:T(128)}, f32[1,128,128]{2,1,0:T(8,128)S(1)}, s32[]{:T(128)}, f32[8,1,128,128]{3,2,1,0:T(8,128)}, s32[]{:T(128)}, /*index=5*/s32[]{:T(128)}) %tuple.85), condition=%wide.region_2.3_spmd.clone, body=%wide.region_1.2_spmd.clone.sunk | while | flops 49156 | bytes 196701 | solution.py:21
  77.8 0.9 add_select_fusion.4
  78.6 0.9 add_select_fusion.4
  79.5 0.9 add_select_fusion.4
  80.4 0.9 add_select_fusion.4
  81.3 0.9 add_select_fusion.4
  82.2 0.9 add_select_fusion.4
  83.0 0.9 add_select_fusion.4
  83.9 0.9 add_select_fusion.4
  84.8 0.9 reduce-window_add_fusion
  86.5 1.2 fusion.76
  87.8 1.9 reverse.3
  89.6 1.9 fusion.26
  91.5 33.6 %all-gather.1 = f32[1024,128]{1,0:T(8,128)} all-gather(f32[128,128]{1,0:T(8,128)S(1)} %get-tuple-element.246), channel_id=3, replica_groups=mesh['parts'=2,'tm'=4,'tile'=2,'chan'=2] {'tm','tile'}, dimensions={0}, use_global_device_ids=true | all-gather | bytes 589824 | tf_op jit(solution)/shard_map/all_gather | solution.py:12
  125.1 7.1 %while.31 = (s32[]{:T(128)}, f32[1,128,128]{2,1,0:T(8,128)S(1)}, s32[]{:T(128)}, f32[8,1,128,128]{3,2,1,0:T(8,128)}, s32[]{:T(128)}, /*index=5*/s32[]{:T(128)}, s32[]{:T(128)}, s32[]{:T(128)}) while((s32[]{:T(128)}, f32[1,128,128]{2,1,0:T(8,128)S(1)}, s32[]{:T(128)}, f32[8,1,128,128]{3,2,1,0:T(8,128)}, s32[]{:T(128)}, ...), condition=%wide.region_6.7_spmd.clone, body=%wide.region_5.6_spmd.clone.sunk | while | flops 49160 | bytes 196763 | solution.py:21
  125.1 0.9 add_select_fusion.5
  126.0 0.9 add_select_fusion.5
  126.9 0.9 add_select_fusion.5
  127.7 0.9 add_select_fusion.5
  128.6 0.9 add_select_fusion.5
  129.5 0.9 add_select_fusion.5
  130.4 0.9 add_select_fusion.5
  131.3 0.9 add_select_fusion.5
  132.2 1.2 reverse_add_fusion
  133.5 1.1 fusion.4
  134.6 1.0 fusion.5
  136.4 0.6 copy-done.5
  137.0 1.1 fusion.3
  139.8 0.9 copy-done.4
  145.2 0.7 pad_maximum_fusion
  146.1 1.1 fusion.6
  147.7 13.6 %all_to_all.65 = bf16[8,384,128]{2,0,1:T(8,128)(2,1)S(1)} all-to-all(bf16[8,384,128]{2,0,1:T(8,128)(2,1)S(1)} %copy.70), channel_id=1, replica_groups=mesh['parts'=2,'tm'=4,'tile'=2,'chan'=2] {'tile'}, dimensions={1} | all-to-all | bytes 1572864 | tf_op jit(solution)/shard_map/all_to_all | solution.py:206
  161.2 1.0 copy.72
  162.3 60.8 %all-reduce.5.cloned.1.call-done = (f32[9,128,128]{2,1,0:T(8,128)}, f32[3,1,128,128]{3,2,1,0:T(8,128)}) async-done(((f32[9,128,128]{2,1,0:T(8,128)}, f32[3,1,128,128]{3,2,1,0:T(8,128)}), (f32[9,128,128]{2,1,0:T(8,128)}, f32[3,1,128,128]{3,2,1,0:T(8,128)})) %all-reduce.5.cloned.1.call-update) | async-done | bytes 786448 | tf_op jit(solution)/shard_map/psum | solution.py:207
  223.0 1.9 copy.143
  224.9 1.6 copy.144
  (58 shorter events, 12.5 us)
Async XLA Ops:
  7.2 8.0 %all-to-all-start.2 = ((s32[2,8,96]{2,1,0:T(8,128)}), s32[2,8,96]{2,1,0:T(8,128)S(1)}, u32[]{:S(2)}, u32[]{:S(2)}) async-start(s32[2,8,96]{2,1,0:T(8,128)} %bitcast.321), calls=%async_computation.2 | async-start | bytes 16384 | tf_op jit(solution)/shard_map/all_to_all | solution.py:167
  15.2 7.0 %all-to-all-start = ((s32[2,8,96]{2,1,0:T(8,128)}), s32[2,8,96]{2,1,0:T(8,128)S(1)}, u32[]{:S(2)}, u32[]{:S(2)}) async-start(s32[2,8,96]{2,1,0:T(8,128)} %bitcast.322), calls=%async_computation | async-start | bytes 16384 | tf_op jit(solution)/shard_map/all_to_all | solution.py:166
  22.2 9.3 %all-to-all-start.1 = ((bf16[16,96,128]{2,1,0:T(8,128)(2,1)}), bf16[16,96,128]{2,1,0:T(8,128)(2,1)S(1)}, u32[]{:S(2)}, u32[]{:S(2)}) async-start(bf16[16,96,128]{2,1,0:T(8,128)(2,1)} %param.11), calls=%async_computation.1 | async-start | bytes 786432 | tf_op jit(solution)/shard_map/all_to_all | solution.py:165
  25.8 10.6 %copy-start.9 = (bf16[9,128,128]{2,1,0:T(8,128)(2,1)S(1)}, bf16[9,128,128]{2,1,0:T(8,128)(2,1)}, u32[]{:S(2)}) copy-start(bf16[9,128,128]{2,1,0:T(8,128)(2,1)} %param.15) | copy-start | bytes 884740
  31.6 54.4 %all-to-all-start.4 = ((bf16[16,192,128]{2,1,0:T(8,128)(2,1)}), bf16[16,192,128]{2,1,0:T(8,128)(2,1)S(1)}, u32[]{:S(2)}, u32[]{:S(2)}) async-start(bf16[16,192,128]{2,1,0:T(8,128)(2,1)} %param.17), calls=%async_computation.4 | async-start | bytes 1572864 | tf_op jit(solution)/shard_map/all_to_all | solution.py:168
  35.1 187.9 %all-reduce.5.cloned.1.call-start = ((), (), s32[]{:S(2)}) async-start(), calls=%async_computation.5 | async-start | bytes 1572864 | tf_op jit(solution)/shard_map/psum | solution.py:207
  39.2 2.1 copy-start.8
  41.6 1.7 copy-start.2
  42.0 0.9 copy-start
  132.2 1.3 copy-start.3
  132.2 2.4 %copy-start.1 = (bf16[8,384,128]{2,1,0:T(8,128)(2,1)S(1)}, bf16[8,384,128]{2,1,0:T(8,128)(2,1)}, u32[]{:S(2)}) copy-start(bf16[8,384,128]{2,1,0:T(8,128)(2,1)} %copy-done) | copy-start | bytes 2359300
  136.0 1.0 copy-start.5
  139.3 1.4 copy-start.4
  144.7 1.3 copy-start.6
  145.1 0.9 copy-start.7
Sparse Core Ops, SparseCore 0:
  146.2 76.8 all-reduce.4
where the time goes:
time: 235 us; the launch traced here: 233 us
  blocking collectives  81.6 us (35%)
  waiting for transfers between devices  73.5 us (31%)
  other arithmetic  20.1 us (9%)
  matrix products  19.2 us (8%)
  starting transfers between devices  14.5 us (6%)
  between operations  14.4 us (6%)
  local copies, waits for them, and re-layouts  9.76 us (4%)
    all_gather x2, blocking collectives, prefix(): everything = lax.all_gather(value, axis)  68 us
    psum x1, waiting for transfers between devices, local(): grad_conv, grad_proj = lax.psum((grad_conv, grad_proj), ('tm', 'tile'))  60.8 us
    select_n x16, other arithmetic, hop(): return jnp.where(reached, new, before)  13.8 us
    all_to_all x1, blocking collectives, local(): lax.all_to_all(whole_out, 'tile', split_axis=1, concat_axis=0, tiled=True)  13.6 us
    unnamed x22, local copies, waits for them, and re-layouts  6.2 us
    all_to_all x1, waiting for transfers between devices, local(): lax.all_to_all(pillar_feat, 'tile', split_axis=0, concat_axis=1, tiled=True)  5.81 us
    dot_general x9, matrix products, forward_local(): jnp.einsum('tywc,cj->tywj', shifted_list[offset], conv_weight[offset], pr...  4.95 us
  transfers between devices with their start and end apart: 5, of which 4 were waited for; matrix products, arithmetic and copies ran while one was open for 8% of the time, Pallas kernels for 0%

commit v1 on v0

v1 whole, which is shorter than its diff:
```python
import functools

import jax
import jax.numpy as jnp
from jax import lax
from jax.experimental import pallas as pl
from jax.experimental.pallas import tpu as pltpu
from jax.sharding import PartitionSpec as P

W = 64
BF = jnp.bfloat16
F32 = jnp.float32
MESH = pl.DeviceIdType.MESH


def mm(a, b, ca=1, cb=0):
    return lax.dot_general(a, b, (((ca,), (cb,)), ((), ())), preferred_element_type=F32)


def body(
    nm, nt, nsweep, per_tile, band,
    feat, cell, count, embed, wconv, proj, dout,
    attn, gconv, gproj,
    fe, ce, ne, cot, emb, x3, feats, deriv, qkv, kvl, cotl, wqkv, ao, g3, cacc, pacc,
    tks, tkr, zks, zkr, gflat, gsend, grecv, gall,
    pil_s, pil_r, loc, tk_s, tk_r, zk_s, zk_r, att_s, att_r, att_l, gs_s, gs_r, ga_s, ga_r,
):
    group = nm * nt
    cells = nt * band
    width = 128
    tm = lax.axis_index("tm")
    tile = lax.axis_index("tile")
    me = tm * nt + tile

    def peer(d):
        return lax.rem(tile + d, nt)

    def gpeer(d):
        return lax.rem(me + d, group)

    def gid(p):
        return {"tm": p // nt, "tile": lax.rem(p, nt)}

    zkr[...] = jnp.zeros_like(zkr)

    barrier = pltpu.get_barrier_semaphore()

    def greet(d, c):
        pl.semaphore_signal(barrier, inc=1, device_id=gid(gpeer(d)), device_id_type=MESH)
        return c

    lax.fori_loop(1, group, greet, 0)
    mine = pl.ds(tile * nsweep, nsweep)
    locals_ = [
        pltpu.make_async_copy(feat.at[mine], fe.at[:, tile], loc.at[0]),
        pltpu.make_async_copy(cell.at[tile], ce.at[tile], loc.at[1]),
        pltpu.make_async_copy(count.at[tile], ne.at[tile], loc.at[2]),
        pltpu.make_async_copy(dout.at[mine], cot.at[:, tile], loc.at[3]),
    ]
    for c in locals_:
        c.start()
    pl.semaphore_wait(barrier, group - 1)

    def pillar_copy(k, to, here, slot):
        theirs = pl.ds(here * nsweep, nsweep)
        src, dst = (
            lambda: (feat.at[theirs], fe.at[:, slot]),
            lambda: (cell.at[here], ce.at[slot]),
            lambda: (count.at[here], ne.at[slot]),
            lambda: (dout.at[theirs], cot.at[:, slot]),
        )[k]()
        return pltpu.make_async_remote_copy(
            src_ref=src, dst_ref=dst, send_sem=pil_s.at[k, to], recv_sem=pil_r.at[k, slot],
            device_id={"tile": to}, device_id_type=MESH,
        )

    def outgoing(k, to):
        return pillar_copy(k, to, to, tile)

    def arrival(k, frm):
        return pillar_copy(k, frm, tile, frm)

    for d in range(1, nt):
        for k in range(3):
            outgoing(k, peer(d)).start()
    for d in range(1, nt):
        outgoing(3, peer(d)).start()

    for i in range(3):
        wqkv[:, i * width:(i + 1) * width] = proj[i, 0]
    emb[...] = embed[...].astype(F32)
    edge = jnp.zeros((nsweep, W, 3 * width), BF)
    x3[:, 0:W, :] = edge
    x3[:, W + cells:2 * W + cells, :] = edge
    g3[...] = jnp.zeros_like(g3)
    cacc[...] = jnp.zeros_like(cacc)
    pacc[...] = jnp.zeros_like(pacc)

    spot = lax.broadcasted_iota(jnp.int32, (band, per_tile), 0)
    col = lax.rem(lax.broadcasted_iota(jnp.int32, (band, width), 0), W)

    def grid_band(s, j):
        row = ce[j, pl.ds(s, 1), :]
        n = ne[j, pl.ds(s, 1), :].astype(F32)
        gate = n / (n + 8.0)
        full = jnp.where(spot == row, gate, 0.0)
        hi = full.astype(BF)
        lo = (full - hi.astype(F32)).astype(BF)
        values = fe[s, j]
        grid = mm(hi, values) + mm(lo, values) + emb[pl.ds(tile * nsweep + s, 1), :]
        mid = grid.astype(BF)
        grid = mid.astype(F32)
        left = jnp.where(col == 0, 0.0, pltpu.roll(grid, 1, 0)).astype(BF)
        right = jnp.where(col == W - 1, 0.0, pltpu.roll(grid, band - 1, 0)).astype(BF)
        rows = pl.ds(pl.multiple_of(W + j * band, W), band)
        x3[s, rows, 0:width] = left
        x3[s, rows, width:2 * width] = mid
        x3[s, rows, 2 * width:3 * width] = right

    for c in locals_:
        c.wait()

    def own_band(s, c):
        grid_band(s, tile)
        return c

    lax.fori_loop(0, nsweep, own_band, 0)
    for d in range(1, nt):
        for k in range(3):
            arrival(k, peer(d)).wait_recv()

    def forward(s, total):
        for d in range(1, nt):
            grid_band(s, peer(d))
        pre = mm(x3[s, 0:cells, :], wconv[0])
        pre = pre + mm(x3[s, W:W + cells, :], wconv[1])
        pre = pre + mm(x3[s, 2 * W:2 * W + cells, :], wconv[2])
        sig = 1.0 / (1.0 + jnp.exp(-pre))
        f = (pre * sig).astype(BF)
        feats[s] = f
        deriv[s] = sig * (1.0 + pre * (1.0 - sig))
        out = mm(f, wqkv[...]).astype(BF)
        qkv[s] = out
        total = total + mm(out[:, width:2 * width], out[:, 2 * width:], 0, 0)
        kvl[s] = total
        return total

    kv_total = lax.fori_loop(0, nsweep, forward, jnp.zeros((width, width), F32))

    def tile_copy(k, to, slot, sem):
        return pltpu.make_async_remote_copy(
            src_ref=tks.at[k], dst_ref=tkr.at[k, slot], send_sem=tk_s.at[k, to],
            recv_sem=tk_r.at[k, sem], device_id={"tile": to}, device_id_type=MESH,
        )

    def block_copy(k, to, slot, sem):
        return pltpu.make_async_remote_copy(
            src_ref=zks.at[k], dst_ref=zkr.at[k, slot], send_sem=zk_s.at[k, to],
            recv_sem=zk_r.at[k, sem], device_id={"tm": to}, device_id_type=MESH,
        )

    def send_tile(k, total):
        low = total.astype(BF)
        tks[k] = low
        tkr[k, tile] = low
        for d in range(1, nt):
            tile_copy(k, peer(d), tile, tile).start()

    def reaches(k, m):
        return (m > tm) if k == 0 else (m < tm)

    def send_block(k):
        for d in range(1, nt):
            tile_copy(k, peer(d), peer(d), peer(d)).wait_recv()
        block = jnp.zeros((width, width), F32)
        inside = jnp.zeros((width, width), F32)
        for i in range(nt):
            part = tkr[k, i].astype(F32)
            block = block + part
            wanted = (i < tile) if k == 0 else (i > tile)
            inside = inside + jnp.where(wanted, part, 0.0)
        zks[k] = block.astype(BF)
        for m in range(nm):
            @pl.when(reaches(k, m))
            def _():
                block_copy(k, m, tm, tm).start()
        return inside

    def take_block(k, inside):
        for m in range(nm):
            @pl.when(reaches(1 - k, m))
            def _():
                block_copy(k, m, m, m).wait_recv()
        for m in range(nm):
            inside = inside + zkr[k, m].astype(F32)
        return inside

    def scale_of(s):
        t = tm * (nsweep * nt) + tile * nsweep + s + 1
        return 1.0 / (jnp.full((1, width), t, jnp.int32).astype(F32) * float(cells))

    send_tile(0, kv_total)
    for d in range(1, nt):
        arrival(3, peer(d)).wait_recv()
    kv_inside = send_block(0)

    def cot_sum(k, total):
        s = nsweep - 1 - k
        total = total + mm(qkv[s, :, 0:width], cot[s].reshape(cells, width), 0, 0) * scale_of(s)
        cotl[s] = total
        return total

    cot_total = lax.fori_loop(0, nsweep, cot_sum, jnp.zeros((width, width), F32))
    send_tile(1, cot_total)
    before = take_block(0, kv_inside)

    def attn_remote(s, to, slot):
        return pltpu.make_async_remote_copy(
            src_ref=ao.at[s, to], dst_ref=attn.at[slot * nsweep + s], send_sem=att_s.at[s, to],
            recv_sem=att_r.at[s, slot], device_id={"tile": to}, device_id_type=MESH,
        )

    def attn_local(s):
        return pltpu.make_async_copy(ao.at[s, tile], attn.at[tile * nsweep + s], att_l.at[s])

    def attend(s, c):
        state = (before + kvl[s]).astype(BF)
        res = mm(qkv[s, :, 0:width], state) * scale_of(s)
        ao[s] = res.astype(BF).reshape(nt, band, width)
        for d in range(1, nt):
            attn_remote(s, peer(d), tile).start()
        attn_local(s).start()
        return c

    cot_inside = send_block(1)
    lax.fori_loop(0, nsweep, attend, 0)
    after = take_block(1, cot_inside)

    def backward(s, c):
        state = (before + kvl[s]).astype(BF)
        adj = (after + cotl[s]).astype(BF)
        gq = (mm(cot[s].reshape(cells, width), state, 1, 1) * scale_of(s)).astype(BF)
        gk = mm(qkv[s, :, 2 * width:3 * width], adj, 1, 1).astype(BF)
        gv = mm(qkv[s, :, width:2 * width], adj).astype(BF)
        g = jnp.concatenate([gq, gk, gv], axis=1)
        pacc[...] += mm(feats[s], g, 0, 0)
        gp = (mm(g, wqkv[...], 1, 1) * deriv[s]).astype(BF)
        g3[0:cells - W, 0:width] = gp[W:]
        g3[:, width:2 * width] = gp
        g3[W:cells, 2 * width:3 * width] = gp[:cells - W]
        cacc[...] += mm(x3[s, W:W + cells, :], g3[...], 0, 0)
        return c

    lax.fori_loop(0, nsweep, backward, 0)

    nconv = 9 * width
    for a in range(3):
        for b in range(3):
            r = (3 * a + b) * width
            gflat[r:r + width] = cacc[b * width:(b + 1) * width, a * width:(a + 1) * width]
    for i in range(3):
        r = nconv + i * width
        gflat[r:r + width] = pacc[:, i * width:(i + 1) * width]
    extra = gflat.shape[0] - 12 * width
    if extra:
        gflat[12 * width:] = jnp.zeros((extra, width), F32)
    gsend[...] = gflat[...].astype(BF).reshape(gsend.shape)

    def part_copy(p, src, slot):
        return pltpu.make_async_remote_copy(
            src_ref=gsend.at[src], dst_ref=grecv.at[slot], send_sem=gs_s.at[p],
            recv_sem=gs_r.at[slot], device_id=gid(p), device_id_type=MESH,
        )

    def sum_copy(p, slot):
        return pltpu.make_async_remote_copy(
            src_ref=gall.at[slot], dst_ref=gall.at[slot], send_sem=ga_s.at[p],
            recv_sem=ga_r.at[slot], device_id=gid(p), device_id_type=MESH,
        )

    def each(fn, start=1):
        def step(d, c):
            fn(gpeer(d))
            return c
        lax.fori_loop(start, group, step, 0)

    each(lambda p: part_copy(p, p, me).start())

    def add_part(d, total):
        p = gpeer(d)
        part_copy(p, p, p).wait_recv()
        return total + grecv[p].astype(F32)

    total = lax.fori_loop(1, group, add_part, gsend[me].astype(F32))
    gall[me] = total.astype(BF)
    each(lambda p: sum_copy(p, me).start())
    each(lambda p: sum_copy(p, p).wait_recv())
    flat = gall[...].reshape(gflat.shape)
    gconv[...] = flat[0:nconv].astype(F32)
    gproj[...] = flat[nconv:12 * width].astype(F32)

    def drain(s, c):
        for d in range(1, nt):
            attn_remote(s, peer(d), tile).wait_send()
            attn_remote(s, peer(d), peer(d)).wait_recv()
        attn_local(s).wait()
        return c

    lax.fori_loop(0, nsweep, drain, 0)
    for d in range(1, nt):
        for k in range(4):
            outgoing(k, peer(d)).wait_send()
        for k in range(2):
            tile_copy(k, peer(d), tile, tile).wait_send()
    for k in range(2):
        for m in range(nm):
            @pl.when(reaches(k, m))
            def _():
                block_copy(k, m, tm, tm).wait_send()
    each(lambda p: part_copy(p, p, me).wait_send())
    each(lambda p: sum_copy(p, me).wait_send())


def local(nm, nt, feat, cell, count, embed, wconv, proj, dout):
    block, per_tile, width = feat.shape
    band = dout.shape[1]
    nsweep = block // nt
    cells = nt * band
    group = nm * nt
    piece = -(-12 * width // (16 * group)) * 16
    vm = pltpu.VMEM
    dma = pltpu.SemaphoreType.DMA
    vspec = pl.BlockSpec(memory_space=pltpu.VMEM)
    aspec = pl.BlockSpec(memory_space=pl.ANY)
    tokens = nsweep * cells
    out = pl.pallas_call(
        functools.partial(body, nm, nt, nsweep, per_tile, band),
        out_shape=(
            jax.ShapeDtypeStruct((block, band, width), BF),
            jax.ShapeDtypeStruct((9 * width, width), F32),
            jax.ShapeDtypeStruct((3 * width, width), F32),
        ),
        in_specs=[aspec, aspec, aspec, vspec, vspec, vspec, aspec],
        out_specs=(aspec, vspec, vspec),
        scratch_shapes=[
            vm((nsweep, nt, per_tile, width), BF),
            vm((nt, nsweep, per_tile), jnp.int32),
            vm((nt, nsweep, per_tile), jnp.int32),
            vm((nsweep, nt, band, width), BF),
            vm((block, width), F32),
            vm((nsweep, cells + 2 * W, 3 * width), BF),
            vm((nsweep, cells, width), BF),
            vm((nsweep, cells, width), F32),
            vm((nsweep, cells, 3 * width), BF),
            vm((nsweep, width, width), F32),
            vm((nsweep, width, width), F32),
            vm((width, 3 * width), BF),
            vm((nsweep, nt, band, width), BF),
            vm((cells, 3 * width), BF),
            vm((3 * width, 3 * width), F32),
            vm((width, 3 * width), F32),
            vm((2, width, width), BF),
            vm((2, nt, width, width), BF),
            vm((2, width, width), BF),
            vm((2, nm, width, width), BF),
            vm((group * piece, width), F32),
            vm((group, piece, width), BF),
            vm((group, piece, width), BF),
            vm((group, piece, width), BF),
            dma((4, nt)), dma((4, nt)), dma((4,)),
            dma((2, nt)), dma((2, nt)), dma((2, nm)), dma((2, nm)),
            dma((nsweep, nt)), dma((nsweep, nt)), dma((nsweep,)),
            dma((group,)), dma((group,)), dma((group,)), dma((group,)),
        ],
        compiler_params=pltpu.CompilerParams(
            collective_id=0, has_side_effects=True, vmem_limit_bytes=48 * 1024 * 1024
        ),
        cost_estimate=pl.CostEstimate(
            flops=2 * tokens * width * width * 36, bytes_accessed=4 * 1024 * 1024,
            transcendentals=tokens * width,
        ),
    )(
        feat, cell.reshape(nt, nsweep, per_tile), count.reshape(nt, nsweep, per_tile),
        embed, wconv.reshape(3, 3 * width, width), proj, dout,
    )
    return (
        out[0],
        out[1].reshape(9, width, width),
        out[2].reshape(3, 1, width, width),
    )


def solution(mesh):
    return jax.shard_map(
        functools.partial(local, mesh.shape["tm"], mesh.shape["tile"]),
        mesh=mesh,
        in_specs=(
            P(("parts", "tm"), "tile", None),
            P(("parts", "tm"), "tile"),
            P(("parts", "tm"), "tile"),
            P(("parts", "tm"), None),
            P(None, None, "chan"),
            P(None, "chan", None, None),
            P(("parts", "tm"), "tile", "chan"),
        ),
        out_specs=(
            P(("parts", "tm"), "tile", "chan"),
            P(None, "parts", "chan"),
            P(None, "chan", "parts", None),
        ),
        check_vma=False,
    )
```

time: 235 us -> 65.5 us (0.28)
  blocking collectives: 81.6 us -> 0 us
  waiting for transfers between devices: 73.5 us -> 0 us
  Pallas kernels: 0 us -> 56.1 us
  other arithmetic: 20.1 us -> 0 us
  matrix products: 19.2 us -> 0 us
  starting transfers between devices: 14.5 us -> 0 us
  between operations: 14.4 us -> 0.66 us
    all_gather x2 -> x0, blocking collectives: 68 us -> none  [prefix(): everything = lax.all_gather(value, axis)]
    psum x1 -> x0, waiting for transfers between devices: 60.8 us -> none  [local(): grad_conv, grad_proj = lax.psum((grad_conv, grad_proj), ('tm', 'tile'))]
    pallas_call x0 -> x1, Pallas kernels: none -> 56.1 us  [local(): pl.pallas_call(functools.partial(body, nm, nt, nsweep, per_tile, band), o...]
    dot_general x34 -> x0, matrix products: 19.2 us -> none  [the longest x9 4.95 us: forward_local(): jnp.einsum('tywc,cj->tywj', shifted_list[offset], conv_weight[offset], pr...]
    all_to_all x4 -> x0, starting transfers between devices: 14.4 us -> none  [the longest x1 4.22 us: local(): lax.all_to_all(pillar_count, 'tile', split_axis=0, concat_axis=1, tiled=T...]
    select_n x16 -> x0, other arithmetic: 13.8 us -> none  [hop(): return jnp.where(reached, new, before)]
    all_to_all x1 -> x0, blocking collectives: 13.6 us -> none  [local(): lax.all_to_all(whole_out, 'tile', split_axis=1, concat_axis=0, tiled=True)]
    all_to_all x4 -> x0, waiting for transfers between devices: 12.7 us -> none  [the longest x1 5.81 us: local(): lax.all_to_all(pillar_feat, 'tile', split_axis=0, concat_axis=1, tiled=True)]
  transfers between devices with their start and end apart: 5 -> 0, of which waited for: 4 -> 0; matrix products, arithmetic and copies ran while one was open for 8% -> 0% of each run, Pallas kernels for 0% -> 0%
where the time goes in v1:
time: 65.5 us; the launch traced here: 65.2 us
  Pallas kernels  56.1 us (86%)
  local copies, waits for them, and re-layouts  8.43 us (13%)
  between operations  0.66 us (1%)
    pallas_call x1, Pallas kernels, local(): pl.pallas_call(functools.partial(body, nm, nt, nsweep, per_tile, band), o...  56.1 us
    unnamed x17, local copies, waits for them, and re-layouts  8.43 us

profile of v1, /device:TPU:0, one launch (start us, length us, event | category | flops | bytes accessed | tf_op | source)
XLA Modules:
  0.0 65.2 jit_solution(525883467172293469)
XLA Ops:
  0.6 0.0 copy-start.6
  0.6 0.7 %copy-done.6 = bf16[16,128]{1,0:T(8,128)(2,1)S(1)} copy-done((bf16[16,128]{1,0:T(8,128)(2,1)S(1)}, bf16[16,128]{1,0:T(8,128)(2,1)}, u32[]{:S(2)}) %copy-start.6) | copy-done | bytes 4120
  1.3 0.0 copy-start
  1.3 1.1 %copy-done = bf16[16,192,128]{2,1,0:T(8,128)(2,1)S(1)} copy-done((bf16[16,192,128]{2,1,0:T(8,128)(2,1)S(1)}, bf16[16,192,128]{2,1,0:T(8,128)(2,1)}, u32[]{:S(2)}) %copy-start) | copy-done | bytes 786456
  2.5 0.0 copy-start.1
  2.5 1.0 %copy-done.1 = bf16[16,96,128]{2,1,0:T(8,128)(2,1)S(1)} copy-done((bf16[16,96,128]{2,1,0:T(8,128)(2,1)S(1)}, bf16[16,96,128]{2,1,0:T(8,128)(2,1)}, u32[]{:S(2)}) %copy-start.1) | copy-done | bytes 393240
  3.5 0.0 copy-start.2
  3.5 1.0 %copy-done.2 = bf16[9,128,128]{2,1,0:T(8,128)(2,1)S(1)} copy-done((bf16[9,128,128]{2,1,0:T(8,128)(2,1)S(1)}, bf16[9,128,128]{2,1,0:T(8,128)(2,1)}, u32[]{:S(2)}) %copy-start.2) | copy-done | bytes 294936
  4.4 0.0 copy-start.3
  4.4 0.9 %copy-done.3 = bf16[3,1,128,128]{3,2,1,0:T(8,128)(2,1)S(1)} copy-done((bf16[3,1,128,128]{3,2,1,0:T(8,128)(2,1)S(1)}, bf16[3,1,128,128]{3,2,1,0:T(8,128)(2,1)}, u32[]{:S(2)}) %copy-start.3) | copy-done | bytes 98328
  5.3 0.0 copy-start.4
  5.3 0.7 %copy-done.4 = s32[16,96]{1,0:T(8,128)S(1)} copy-done((s32[16,96]{1,0:T(8,128)S(1)}, s32[16,96]{1,0:T(8,128)}, u32[]{:S(2)}) %copy-start.4) | copy-done | bytes 6168
  6.0 0.0 copy-start.5
  6.0 0.7 %copy-done.5 = s32[16,96]{1,0:T(8,128)S(1)} copy-done((s32[16,96]{1,0:T(8,128)S(1)}, s32[16,96]{1,0:T(8,128)}, u32[]{:S(2)}) %copy-start.5) | copy-done | bytes 6168
  6.7 56.1 %shard_map.94 = (bf16[16,192,128]{2,1,0:T(8,128)(2,1)S(1)}, f32[1152,128]{1,0:T(8,128)S(1)}, f32[384,128]{1,0:T(8,128)S(1)}) custom-call(bf16[16,96,128]{2,1,0:T(8,128)(2,1)S(1)} %copy-done.1, s32[2,8,96]{2,1,0:T(8,128)S(1)} %bitcast.10, s32[2,8,96]{2,1,0:T(8,128)S(1)} %bitcast.11, bf16[16,128]{1,0:T(8,128)(2,1)S(1)} %copy-done.6, ...), custom_call_target="tpu_custom_call" | custom-call | flops 3623878656 | bytes 4194304 | tf_op jit(solution)/shard_map/pallas_call | solution.py:336
  62.8 0.9 %copy.14 = bf16[16,192,128]{2,1,0:T(8,128)(2,1)} copy(bf16[16,192,128]{2,1,0:T(8,128)(2,1)S(1)} %get-tuple-element.15) | data formatting | bytes 1572864
  63.7 0.8 %copy.15 = f32[9,128,128]{2,1,0:T(8,128)} copy(f32[9,128,128]{2,1,0:T(8,128)S(1)} %bitcast.7) | data formatting | bytes 1179648
  64.5 0.7 %copy.16 = f32[3,1,128,128]{3,2,1,0:T(8,128)} copy(f32[3,1,128,128]{3,2,1,0:T(8,128)S(1)} %bitcast.8) | data formatting | bytes 393216
Async XLA Ops:
  0.6 0.7 %copy-start.6 = (bf16[16,128]{1,0:T(8,128)(2,1)S(1)}, bf16[16,128]{1,0:T(8,128)(2,1)}, u32[]{:S(2)}) copy-start(bf16[16,128]{1,0:T(8,128)(2,1)} %embed.1) | copy-start | bytes 12292
  1.3 1.1 %copy-start = (bf16[16,192,128]{2,1,0:T(8,128)(2,1)S(1)}, bf16[16,192,128]{2,1,0:T(8,128)(2,1)}, u32[]{:S(2)}) copy-start(bf16[16,192,128]{2,1,0:T(8,128)(2,1)} %dout.1) | copy-start | bytes 2359300
  2.5 1.0 %copy-start.1 = (bf16[16,96,128]{2,1,0:T(8,128)(2,1)S(1)}, bf16[16,96,128]{2,1,0:T(8,128)(2,1)}, u32[]{:S(2)}) copy-start(bf16[16,96,128]{2,1,0:T(8,128)(2,1)} %feat.1) | copy-start | bytes 1179652
  3.5 1.0 %copy-start.2 = (bf16[9,128,128]{2,1,0:T(8,128)(2,1)S(1)}, bf16[9,128,128]{2,1,0:T(8,128)(2,1)}, u32[]{:S(2)}) copy-start(bf16[9,128,128]{2,1,0:T(8,128)(2,1)} %param.11) | copy-start | bytes 884740
  4.4 0.9 %copy-start.3 = (bf16[3,1,128,128]{3,2,1,0:T(8,128)(2,1)S(1)}, bf16[3,1,128,128]{3,2,1,0:T(8,128)(2,1)}, u32[]{:S(2)}) copy-start(bf16[3,1,128,128]{3,2,1,0:T(8,128)(2,1)} %proj.1) | copy-start | bytes 294916
  5.3 0.7 %copy-start.4 = (s32[16,96]{1,0:T(8,128)S(1)}, s32[16,96]{1,0:T(8,128)}, u32[]{:S(2)}) copy-start(s32[16,96]{1,0:T(8,128)} %param.8) | copy-start | bytes 18436
  6.0 0.7 %copy-start.5 = (s32[16,96]{1,0:T(8,128)S(1)}, s32[16,96]{1,0:T(8,128)}, u32[]{:S(2)}) copy-start(s32[16,96]{1,0:T(8,128)} %param.9) | copy-start | bytes 18436

commit v2 on v1

--- a/solution.py
+++ b/solution.py
@@ -19,9 +19,9 @@
 
 def body(
     nm, nt, nsweep, per_tile, band,
-    feat, cell, count, embed, wconv, proj, dout,
+    feat, cell, count, embed_in, wconv_in, proj_in, dout,
     attn, gconv, gproj,
-    fe, ce, ne, cot, emb, x3, feats, deriv, qkv, kvl, cotl, wqkv, ao, g3, cacc, pacc,
+    embed, wconv, proj, fe, ce, ne, cot, emb, x3, feats, deriv, qkv, kvl, cotl, wqkv, ao, g3, cacc, pacc,
     tks, tkr, zks, zkr, gflat, gsend, grecv, gall,
     pil_s, pil_r, loc, tk_s, tk_r, zk_s, zk_r, att_s, att_r, att_l, gs_s, gs_r, ga_s, ga_r,
 ):
@@ -55,10 +55,19 @@
         pltpu.make_async_copy(feat.at[mine], fe.at[:, tile], loc.at[0]),
         pltpu.make_async_copy(cell.at[tile], ce.at[tile], loc.at[1]),
         pltpu.make_async_copy(count.at[tile], ne.at[tile], loc.at[2]),
-        pltpu.make_async_copy(dout.at[mine], cot.at[:, tile], loc.at[3]),
+        pltpu.make_async_copy(embed_in, embed, loc.at[3]),
+        pltpu.make_async_copy(wconv_in, wconv, loc.at[4]),
+        pltpu.make_async_copy(proj_in, proj, loc.at[5]),
+        pltpu.make_async_copy(dout.at[mine], cot.at[:, tile], loc.at[6]),
     ]
     for c in locals_:
         c.start()
+    edge = jnp.zeros((nsweep, W, 3 * width), BF)
+    x3[:, 0:W, :] = edge
+    x3[:, W + cells:2 * W + cells, :] = edge
+    g3[...] = jnp.zeros_like(g3)
+    cacc[...] = jnp.zeros_like(cacc)
+    pacc[...] = jnp.zeros_like(pacc)
     pl.semaphore_wait(barrier, group - 1)
 
     def pillar_copy(k, to, here, slot):
@@ -86,15 +95,6 @@
     for d in range(1, nt):
         outgoing(3, peer(d)).start()
 
-    for i in range(3):
-        wqkv[:, i * width:(i + 1) * width] = proj[i, 0]
-    emb[...] = embed[...].astype(F32)
-    edge = jnp.zeros((nsweep, W, 3 * width), BF)
-    x3[:, 0:W, :] = edge
-    x3[:, W + cells:2 * W + cells, :] = edge
-    g3[...] = jnp.zeros_like(g3)
-    cacc[...] = jnp.zeros_like(cacc)
-    pacc[...] = jnp.zeros_like(pacc)
 
     spot = lax.broadcasted_iota(jnp.int32, (band, per_tile), 0)
     col = lax.rem(lax.broadcasted_iota(jnp.int32, (band, width), 0), W)
@@ -117,8 +117,11 @@
         x3[s, rows, width:2 * width] = mid
         x3[s, rows, 2 * width:3 * width] = right
 
-    for c in locals_:
+    for c in locals_[:6]:
         c.wait()
+    for i in range(3):
+        wqkv[:, i * width:(i + 1) * width] = proj[i, 0]
+    emb[...] = embed[...].astype(F32)
 
     def own_band(s, c):
         grid_band(s, tile)
@@ -200,9 +203,10 @@
         return 1.0 / (jnp.full((1, width), t, jnp.int32).astype(F32) * float(cells))
 
     send_tile(0, kv_total)
+    kv_inside = send_block(0)
+    locals_[6].wait()
     for d in range(1, nt):
         arrival(3, peer(d)).wait_recv()
-    kv_inside = send_block(0)
 
     def cot_sum(k, total):
         s = nsweep - 1 - k
@@ -332,6 +336,7 @@
     dma = pltpu.SemaphoreType.DMA
     vspec = pl.BlockSpec(memory_space=pltpu.VMEM)
     aspec = pl.BlockSpec(memory_space=pl.ANY)
+    hspec = pl.BlockSpec(memory_space=pltpu.HBM)
     tokens = nsweep * cells
     out = pl.pallas_call(
         functools.partial(body, nm, nt, nsweep, per_tile, band),
@@ -340,9 +345,12 @@
             jax.ShapeDtypeStruct((9 * width, width), F32),
             jax.ShapeDtypeStruct((3 * width, width), F32),
         ),
-        in_specs=[aspec, aspec, aspec, vspec, vspec, vspec, aspec],
+        in_specs=[hspec] * 7,
         out_specs=(aspec, vspec, vspec),
         scratch_shapes=[
+            vm((block, width), BF),
+            vm((3, 3 * width, width), BF),
+            vm((3, 1, width, width), BF),
             vm((nsweep, nt, per_tile, width), BF),
             vm((nt, nsweep, per_tile), jnp.int32),
             vm((nt, nsweep, per_tile), jnp.int32),
@@ -367,13 +375,13 @@
             vm((group, piece, width), BF),
             vm((group, piece, width), BF),
             vm((group, piece, width), BF),
-            dma((4, nt)), dma((4, nt)), dma((4,)),
+            dma((4, nt)), dma((4, nt)), dma((7,)),
             dma((2, nt)), dma((2, nt)), dma((2, nm)), dma((2, nm)),
             dma((nsweep, nt)), dma((nsweep, nt)), dma((nsweep,)),
             dma((group,)), dma((group,)), dma((group,)), dma((group,)),
         ],
         compiler_params=pltpu.CompilerParams(
-            collective_id=0, has_side_effects=True, vmem_limit_bytes=48 * 1024 * 1024
+            collective_id=0, has_side_effects=True, vmem_limit_bytes=65000 * 1024
         ),
         cost_estimate=pl.CostEstimate(
             flops=2 * tokens * width * width * 36, bytes_accessed=4 * 1024 * 1024,

time: 65.5 us -> 64 us (0.977)
  local copies, waits for them, and re-layouts: 8.43 us -> 3.93 us
  Pallas kernels: 56.1 us -> 59.2 us
    unnamed x17 -> x7, local copies, waits for them, and re-layouts: 8.43 us -> 3.93 us
    pallas_call x1, Pallas kernels: 56.1 us -> 59.2 us  [local(): pl.pallas_call(functools.partial(body, nm, nt, nsweep, per_tile, band), o...]
where the time goes in v2:
time: 64 us; the launch traced here: 63.8 us
  Pallas kernels  59.2 us (92%)
  local copies, waits for them, and re-layouts  3.93 us (6%)
  between operations  0.65 us (1%)
    pallas_call x1, Pallas kernels, local(): pl.pallas_call(functools.partial(body, nm, nt, nsweep, per_tile, band), o...  59.2 us
    unnamed x7, local copies, waits for them, and re-layouts  3.93 us

profile of v2, /device:TPU:0, one launch (start us, length us, event | category | flops | bytes accessed | tf_op | source)
XLA Modules:
  0.0 63.8 jit_solution(5083001277230217470)
XLA Ops:
  0.6 59.2 %shard_map.94 = (bf16[16,192,128]{2,1,0:T(8,128)(2,1)}, f32[1152,128]{1,0:T(8,128)}, f32[384,128]{1,0:T(8,128)}) custom-call(bf16[16,96,128]{2,1,0:T(8,128)(2,1)} %feat.1, s32[2,8,96]{2,1,0:T(8,128)} %bitcast.10, s32[2,8,96]{2,1,0:T(8,128)} %bitcast.11, bf16[16,128]{1,0:T(8,128)(2,1)} %embed_in.1, bf16[3,384,128]{2,1,0:T(8,128)(2,1)} %bitcast.9, ...), custom_call_target="tpu_custom_call" | custom-call | flops 3623878656 | bytes 4194304 | tf_op jit(solution)/shard_map/pallas_call | solution.py:341
  59.8 0.0 copy-start
  59.9 2.1 %copy.14 = bf16[16,192,128]{2,1,0:T(8,128)(2,1)} copy(bf16[16,192,128]{2,1,0:T(8,128)(2,1)} %get-tuple-element.15) | data formatting | bytes 1572864
  62.0 0.0 copy-done
  62.0 0.0 copy-start.1
  62.0 0.8 %copy.15 = f32[9,128,128]{2,1,0:T(8,128)} copy(f32[9,128,128]{2,1,0:T(8,128)S(1)} %bitcast.7) | data formatting | bytes 1179648
  62.8 0.3 copy-done.1
  63.1 0.7 %copy.16 = f32[3,1,128,128]{3,2,1,0:T(8,128)} copy(f32[3,1,128,128]{3,2,1,0:T(8,128)S(1)} %bitcast.8) | data formatting | bytes 393216
Async XLA Ops:
  59.8 2.1 %copy-start = (f32[1152,128]{1,0:T(8,128)S(1)}, f32[1152,128]{1,0:T(8,128)}, u32[]{:S(2)}) copy-start(f32[1152,128]{1,0:T(8,128)} %get-tuple-element.7) | copy-start | bytes 1769476
  62.0 1.1 %copy-start.1 = (f32[384,128]{1,0:T(8,128)S(1)}, f32[384,128]{1,0:T(8,128)}, u32[]{:S(2)}) copy-start(f32[384,128]{1,0:T(8,128)} %get-tuple-element.8) | copy-start | bytes 589828

commit v3 on v2

--- a/solution.py
+++ b/solution.py
@@ -21,7 +21,7 @@
     nm, nt, nsweep, per_tile, band,
     feat, cell, count, embed_in, wconv_in, proj_in, dout,
     attn, gconv, gproj,
-    embed, wconv, proj, fe, ce, ne, cot, emb, x3, feats, deriv, qkv, kvl, cotl, wqkv, ao, g3, cacc, pacc,
+    embed, wconv, proj, fe, ce, ne, cot, emb, x3, feats, gqs, deriv, qkv, kvl, cotl, wqkv, ao, g3, cacc, pacc,
     tks, tkr, zks, zkr, gflat, gsend, grecv, gall,
     pil_s, pil_r, loc, tk_s, tk_r, zk_s, zk_r, att_s, att_r, att_l, gs_s, gs_r, ga_s, ga_r,
 ):
@@ -92,8 +92,6 @@
     for d in range(1, nt):
         for k in range(3):
             outgoing(k, peer(d)).start()
-    for d in range(1, nt):
-        outgoing(3, peer(d)).start()
 
 
     spot = lax.broadcasted_iota(jnp.int32, (band, per_tile), 0)
@@ -127,10 +125,12 @@
         grid_band(s, tile)
         return c
 
-    lax.fori_loop(0, nsweep, own_band, 0)
+    lax.fori_loop(0, nsweep, own_band, 0, unroll=2)
     for d in range(1, nt):
         for k in range(3):
             arrival(k, peer(d)).wait_recv()
+    for d in range(1, nt):
+        outgoing(3, peer(d)).start()
 
     def forward(s, total):
         for d in range(1, nt):
@@ -148,7 +148,7 @@
         kvl[s] = total
         return total
 
-    kv_total = lax.fori_loop(0, nsweep, forward, jnp.zeros((width, width), F32))
+    kv_total = lax.fori_loop(0, nsweep, forward, jnp.zeros((width, width), F32), unroll=2)
 
     def tile_copy(k, to, slot, sem):
         return pltpu.make_async_remote_copy(
@@ -214,7 +214,7 @@
         cotl[s] = total
         return total
 
-    cot_total = lax.fori_loop(0, nsweep, cot_sum, jnp.zeros((width, width), F32))
+    cot_total = lax.fori_loop(0, nsweep, cot_sum, jnp.zeros((width, width), F32), unroll=2)
     send_tile(1, cot_total)
     before = take_block(0, kv_inside)
 
@@ -234,28 +234,28 @@
         for d in range(1, nt):
             attn_remote(s, peer(d), tile).start()
         attn_local(s).start()
+        gqs[s] = (mm(cot[s].reshape(cells, width), state, 1, 1) * scale_of(s)).astype(BF)
         return c
 
     cot_inside = send_block(1)
-    lax.fori_loop(0, nsweep, attend, 0)
+    lax.fori_loop(0, nsweep, attend, 0, unroll=2)
     after = take_block(1, cot_inside)
 
     def backward(s, c):
-        state = (before + kvl[s]).astype(BF)
         adj = (after + cotl[s]).astype(BF)
-        gq = (mm(cot[s].reshape(cells, width), state, 1, 1) * scale_of(s)).astype(BF)
         gk = mm(qkv[s, :, 2 * width:3 * width], adj, 1, 1).astype(BF)
         gv = mm(qkv[s, :, width:2 * width], adj).astype(BF)
-        g = jnp.concatenate([gq, gk, gv], axis=1)
+        g = jnp.concatenate([gqs[s], gk, gv], axis=1)
         pacc[...] += mm(feats[s], g, 0, 0)
         gp = (mm(g, wqkv[...], 1, 1) * deriv[s]).astype(BF)
-        g3[0:cells - W, 0:width] = gp[W:]
-        g3[:, width:2 * width] = gp
-        g3[W:cells, 2 * width:3 * width] = gp[:cells - W]
-        cacc[...] += mm(x3[s, W:W + cells, :], g3[...], 0, 0)
+        slot = lax.rem(s, 2)
+        g3[slot, 0:cells - W, 0:width] = gp[W:]
+        g3[slot, :, width:2 * width] = gp
+        g3[slot, W:cells, 2 * width:3 * width] = gp[:cells - W]
+        cacc[...] += mm(x3[s, W:W + cells, :], g3[slot], 0, 0)
         return c
 
-    lax.fori_loop(0, nsweep, backward, 0)
+    lax.fori_loop(0, nsweep, backward, 0, unroll=2)
 
     nconv = 9 * width
     for a in range(3):
@@ -358,13 +358,14 @@
             vm((block, width), F32),
             vm((nsweep, cells + 2 * W, 3 * width), BF),
             vm((nsweep, cells, width), BF),
+            vm((nsweep, cells, width), BF),
             vm((nsweep, cells, width), F32),
             vm((nsweep, cells, 3 * width), BF),
             vm((nsweep, width, width), F32),
             vm((nsweep, width, width), F32),
             vm((width, 3 * width), BF),
             vm((nsweep, nt, band, width), BF),
-            vm((cells, 3 * width), BF),
+            vm((2, cells, 3 * width), BF),
             vm((3 * width, 3 * width), F32),
             vm((width, 3 * width), F32),
             vm((2, width, width), BF),

time: 64 us -> 58.9 us (0.920)
  Pallas kernels: 59.2 us -> 54.1 us
    pallas_call x1, Pallas kernels: 59.2 us -> 54.1 us  [local(): pl.pallas_call(functools.partial(body, nm, nt, nsweep, per_tile, band), o...]
where the time goes in v3:
time: 58.9 us; the launch traced here: 58.7 us
  Pallas kernels  54.1 us (92%)
  local copies, waits for them, and re-layouts  3.93 us (7%)
  between operations  0.65 us (1%)
    pallas_call x1, Pallas kernels, local(): pl.pallas_call(functools.partial(body, nm, nt, nsweep, per_tile, band), o...  54.1 us
    unnamed x7, local copies, waits for them, and re-layouts  3.93 us

profile of v3, /device:TPU:0, one launch (start us, length us, event | category | flops | bytes accessed | tf_op | source)
XLA Modules:
  0.0 58.7 jit_solution(16728583806774133013)
XLA Ops:
  0.6 54.1 %shard_map.94 = (bf16[16,192,128]{2,1,0:T(8,128)(2,1)}, f32[1152,128]{1,0:T(8,128)}, f32[384,128]{1,0:T(8,128)}) custom-call(bf16[16,96,128]{2,1,0:T(8,128)(2,1)} %feat.1, s32[2,8,96]{2,1,0:T(8,128)} %bitcast.10, s32[2,8,96]{2,1,0:T(8,128)} %bitcast.11, bf16[16,128]{1,0:T(8,128)(2,1)} %embed_in.1, bf16[3,384,128]{2,1,0:T(8,128)(2,1)} %bitcast.9, ...), custom_call_target="tpu_custom_call" | custom-call | flops 3623878656 | bytes 4194304 | tf_op jit(solution)/shard_map/pallas_call | solution.py:341
  54.8 0.0 copy-start
  54.8 2.1 %copy.14 = bf16[16,192,128]{2,1,0:T(8,128)(2,1)} copy(bf16[16,192,128]{2,1,0:T(8,128)(2,1)} %get-tuple-element.15) | data formatting | bytes 1572864
  56.9 0.0 copy-done
  56.9 0.0 copy-start.1
  56.9 0.8 %copy.15 = f32[9,128,128]{2,1,0:T(8,128)} copy(f32[9,128,128]{2,1,0:T(8,128)S(1)} %bitcast.7) | data formatting | bytes 1179648
  57.7 0.3 copy-done.1
  58.0 0.7 %copy.16 = f32[3,1,128,128]{3,2,1,0:T(8,128)} copy(f32[3,1,128,128]{3,2,1,0:T(8,128)S(1)} %bitcast.8) | data formatting | bytes 393216
Async XLA Ops:
  54.8 2.1 %copy-start = (f32[1152,128]{1,0:T(8,128)S(1)}, f32[1152,128]{1,0:T(8,128)}, u32[]{:S(2)}) copy-start(f32[1152,128]{1,0:T(8,128)} %get-tuple-element.7) | copy-start | bytes 1769476
  56.9 1.1 %copy-start.1 = (f32[384,128]{1,0:T(8,128)S(1)}, f32[384,128]{1,0:T(8,128)}, u32[]{:S(2)}) copy-start(f32[384,128]{1,0:T(8,128)} %get-tuple-element.8) | copy-start | bytes 589828

commit v4 on v3

--- a/solution.py
+++ b/solution.py
@@ -22,7 +22,7 @@
     feat, cell, count, embed_in, wconv_in, proj_in, dout,
     attn, gconv, gproj,
     embed, wconv, proj, fe, ce, ne, cot, emb, x3, feats, gqs, deriv, qkv, kvl, cotl, wqkv, ao, g3, cacc, pacc,
-    tks, tkr, zks, zkr, gflat, gsend, grecv, gall,
+    tks, tkr, zks, zkr, gflats, gsends, grecvs, galls,
     pil_s, pil_r, loc, tk_s, tk_r, zk_s, zk_r, att_s, att_r, att_l, gs_s, gs_r, ga_s, ga_r,
 ):
     group = nm * nt
@@ -65,7 +65,8 @@
     edge = jnp.zeros((nsweep, W, 3 * width), BF)
     x3[:, 0:W, :] = edge
     x3[:, W + cells:2 * W + cells, :] = edge
-    g3[...] = jnp.zeros_like(g3)
+    g3[:, cells - W:cells, 0:width] = edge[:, :, 0:width]
+    g3[:, 0:W, 2 * width:3 * width] = edge[:, :, 0:width]
     cacc[...] = jnp.zeros_like(cacc)
     pacc[...] = jnp.zeros_like(pacc)
     pl.semaphore_wait(barrier, group - 1)
@@ -248,60 +249,72 @@
         g = jnp.concatenate([gqs[s], gk, gv], axis=1)
         pacc[...] += mm(feats[s], g, 0, 0)
         gp = (mm(g, wqkv[...], 1, 1) * deriv[s]).astype(BF)
-        slot = lax.rem(s, 2)
-        g3[slot, 0:cells - W, 0:width] = gp[W:]
-        g3[slot, :, width:2 * width] = gp
-        g3[slot, W:cells, 2 * width:3 * width] = gp[:cells - W]
-        cacc[...] += mm(x3[s, W:W + cells, :], g3[slot], 0, 0)
+        g3[s, 0:cells - W, 0:width] = gp[W:]
+        g3[s, :, width:2 * width] = gp
+        g3[s, W:cells, 2 * width:3 * width] = gp[:cells - W]
+        return c
+
+    def conv_part(s, c):
+        cacc[...] += mm(x3[s, W:W + cells, :], g3[s], 0, 0)
         return c
 
     lax.fori_loop(0, nsweep, backward, 0, unroll=2)
 
-    nconv = 9 * width
-    for a in range(3):
-        for b in range(3):
-            r = (3 * a + b) * width
-            gflat[r:r + width] = cacc[b * width:(b + 1) * width, a * width:(a + 1) * width]
-    for i in range(3):
-        r = nconv + i * width
-        gflat[r:r + width] = pacc[:, i * width:(i + 1) * width]
-    extra = gflat.shape[0] - 12 * width
-    if extra:
-        gflat[12 * width:] = jnp.zeros((extra, width), F32)
-    gsend[...] = gflat[...].astype(BF).reshape(gsend.shape)
-
-    def part_copy(p, src, slot):
-        return pltpu.make_async_remote_copy(
-            src_ref=gsend.at[src], dst_ref=grecv.at[slot], send_sem=gs_s.at[p],
-            recv_sem=gs_r.at[slot], device_id=gid(p), device_id_type=MESH,
-        )
-
-    def sum_copy(p, slot):
-        return pltpu.make_async_remote_copy(
-            src_ref=gall.at[slot], dst_ref=gall.at[slot], send_sem=ga_s.at[p],
-            recv_sem=ga_r.at[slot], device_id=gid(p), device_id_type=MESH,
-        )
-
-    def each(fn, start=1):
+    def part_copy(k, p, src, slot):
+        return pltpu.make_async_remote_copy(
+            src_ref=gsends[k].at[src], dst_ref=grecvs[k].at[slot], send_sem=gs_s.at[k, p],
+            recv_sem=gs_r.at[k, slot], device_id=gid(p), device_id_type=MESH,
+        )
+
+    def sum_copy(k, p, slot):
+        return pltpu.make_async_remote_copy(
+            src_ref=galls[k].at[slot], dst_ref=galls[k].at[slot], send_sem=ga_s.at[k, p],
+            recv_sem=ga_r.at[k, slot], device_id=gid(p), device_id_type=MESH,
+        )
+
+    def each(fn):
         def step(d, c):
             fn(gpeer(d))
             return c
-        lax.fori_loop(start, group, step, 0)
-
-    each(lambda p: part_copy(p, p, me).start())
-
-    def add_part(d, total):
-        p = gpeer(d)
-        part_copy(p, p, p).wait_recv()
-        return total + grecv[p].astype(F32)
-
-    total = lax.fori_loop(1, group, add_part, gsend[me].astype(F32))
-    gall[me] = total.astype(BF)
-    each(lambda p: sum_copy(p, me).start())
-    each(lambda p: sum_copy(p, p).wait_recv())
-    flat = gall[...].reshape(gflat.shape)
-    gconv[...] = flat[0:nconv].astype(F32)
-    gproj[...] = flat[nconv:12 * width].astype(F32)
+        lax.fori_loop(1, group, step, 0)
+
+    def send_parts(k, blocks):
+        gflat = gflats[k]
+        for i, block in enumerate(blocks):
+            gflat[i * width:(i + 1) * width] = block
+        used = len(blocks) * width
+        if gflat.shape[0] > used:
+            gflat[used:] = jnp.zeros((gflat.shape[0] - used, width), F32)
+        gsends[k][...] = gflat[...].astype(BF).reshape(gsends[k].shape)
+        each(lambda p: part_copy(k, p, p, me).start())
+
+    def send_sums(k):
+        def add_part(d, total):
+            p = gpeer(d)
+            part_copy(k, p, p, p).wait_recv()
+            return total + grecvs[k][p].astype(F32)
+
+        total = lax.fori_loop(1, group, add_part, gsends[k][me].astype(F32))
+        galls[k][me] = total.astype(BF)
+        each(lambda p: sum_copy(k, p, me).start())
+
+    def finish(k, out):
+        each(lambda p: sum_copy(k, p, p).wait_recv())
+        flat = galls[k][...].reshape(gflats[k].shape)
+        out[...] = flat[0:out.shape[0]].astype(F32)
+
+    send_parts(0, [pacc[:, i * width:(i + 1) * width] for i in range(3)])
+    half = nsweep // 2
+    lax.fori_loop(0, half, conv_part, 0, unroll=min(2, max(half, 1)))
+    send_sums(0)
+    lax.fori_loop(half, nsweep, conv_part, 0, unroll=min(2, nsweep - half))
+    send_parts(1, [
+        cacc[b * width:(b + 1) * width, a * width:(a + 1) * width]
+        for a in range(3) for b in range(3)
+    ])
+    finish(0, gproj)
+    send_sums(1)
+    finish(1, gconv)
 
     def drain(s, c):
         for d in range(1, nt):
@@ -321,8 +334,9 @@
             @pl.when(reaches(k, m))
             def _():
                 block_copy(k, m, tm, tm).wait_send()
-    each(lambda p: part_copy(p, p, me).wait_send())
-    each(lambda p: sum_copy(p, me).wait_send())
+    for k in range(2):
+        each(lambda p: part_copy(k, p, p, me).wait_send())
+        each(lambda p: sum_copy(k, p, me).wait_send())
 
 
 def local(nm, nt, feat, cell, count, embed, wconv, proj, dout):
@@ -331,7 +345,7 @@
     nsweep = block // nt
     cells = nt * band
     group = nm * nt
-    piece = -(-12 * width // (16 * group)) * 16
+    pieces = [-(-n * width // (16 * group)) * 16 for n in (3, 9)]
     vm = pltpu.VMEM
     dma = pltpu.SemaphoreType.DMA
     vspec = pl.BlockSpec(memory_space=pltpu.VMEM)
@@ -365,21 +379,21 @@
             vm((nsweep, width, width), F32),
             vm((width, 3 * width), BF),
             vm((nsweep, nt, band, width), BF),
-            vm((2, cells, 3 * width), BF),
+            vm((nsweep, cells, 3 * width), BF),
             vm((3 * width, 3 * width), F32),
             vm((width, 3 * width), F32),
             vm((2, width, width), BF),
             vm((2, nt, width, width), BF),
             vm((2, width, width), BF),
             vm((2, nm, width, width), BF),
-            vm((group * piece, width), F32),
-            vm((group, piece, width), BF),
-            vm((group, piece, width), BF),
-            vm((group, piece, width), BF),
+            [vm((group * p, width), F32) for p in pieces],
+            [vm((group, p, width), BF) for p in pieces],
+            [vm((group, p, width), BF) for p in pieces],
+            [vm((group, p, width), BF) for p in pieces],
             dma((4, nt)), dma((4, nt)), dma((7,)),
             dma((2, nt)), dma((2, nt)), dma((2, nm)), dma((2, nm)),
             dma((nsweep, nt)), dma((nsweep, nt)), dma((nsweep,)),
-            dma((group,)), dma((group,)), dma((group,)), dma((group,)),
+            dma((2, group)), dma((2, group)), dma((2, group)), dma((2, group)),
         ],
         compiler_params=pltpu.CompilerParams(
             collective_id=0, has_side_effects=True, vmem_limit_bytes=65000 * 1024

time: 58.9 us -> 61.8 us (1.049)
  Pallas kernels: 54.1 us -> 57 us
    pallas_call x1, Pallas kernels: 54.1 us -> 57 us  [local(): pl.pallas_call(functools.partial(body, nm, nt, nsweep, per_tile, band), o...]
where the time goes in v4:
time: 61.8 us; the launch traced here: 61.6 us
  Pallas kernels  57 us (92%)
  local copies, waits for them, and re-layouts  3.93 us (6%)
  between operations  0.65 us (1%)
    pallas_call x1, Pallas kernels, local(): pl.pallas_call(functools.partial(body, nm, nt, nsweep, per_tile, band), o...  57 us
    unnamed x7, local copies, waits for them, and re-layouts  3.93 us

profile of v4, /device:TPU:0, one launch (start us, length us, event | category | flops | bytes accessed | tf_op | source)
XLA Modules:
  0.0 61.6 jit_solution(13266278138201919894)
XLA Ops:
  0.6 57.0 %shard_map.94 = (bf16[16,192,128]{2,1,0:T(8,128)(2,1)}, f32[1152,128]{1,0:T(8,128)}, f32[384,128]{1,0:T(8,128)}) custom-call(bf16[16,96,128]{2,1,0:T(8,128)(2,1)} %feat.1, s32[2,8,96]{2,1,0:T(8,128)} %bitcast.10, s32[2,8,96]{2,1,0:T(8,128)} %bitcast.11, bf16[16,128]{1,0:T(8,128)(2,1)} %embed_in.1, bf16[3,384,128]{2,1,0:T(8,128)(2,1)} %bitcast.9, ...), custom_call_target="tpu_custom_call" | custom-call | flops 3623878656 | bytes 4194304 | tf_op jit(solution)/shard_map/pallas_call | solution.py:355
  57.7 0.0 copy-start
  57.7 2.1 %copy.14 = bf16[16,192,128]{2,1,0:T(8,128)(2,1)} copy(bf16[16,192,128]{2,1,0:T(8,128)(2,1)} %get-tuple-element.15) | data formatting | bytes 1572864
  59.8 0.0 copy-done
  59.8 0.0 copy-start.1
  59.8 0.8 %copy.15 = f32[9,128,128]{2,1,0:T(8,128)} copy(f32[9,128,128]{2,1,0:T(8,128)S(1)} %bitcast.7) | data formatting | bytes 1179648
  60.6 0.3 copy-done.1
  60.9 0.7 %copy.16 = f32[3,1,128,128]{3,2,1,0:T(8,128)} copy(f32[3,1,128,128]{3,2,1,0:T(8,128)S(1)} %bitcast.8) | data formatting | bytes 393216
Async XLA Ops:
  57.7 2.1 %copy-start = (f32[1152,128]{1,0:T(8,128)S(1)}, f32[1152,128]{1,0:T(8,128)}, u32[]{:S(2)}) copy-start(f32[1152,128]{1,0:T(8,128)} %get-tuple-element.7) | copy-start | bytes 1769476
  59.8 1.1 %copy-start.1 = (f32[384,128]{1,0:T(8,128)S(1)}, f32[384,128]{1,0:T(8,128)}, u32[]{:S(2)}) copy-start(f32[384,128]{1,0:T(8,128)} %get-tuple-element.8) | copy-start | bytes 589828

commit v5 on v3

--- a/solution.py
+++ b/solution.py
@@ -125,7 +125,7 @@
         grid_band(s, tile)
         return c
 
-    lax.fori_loop(0, nsweep, own_band, 0, unroll=2)
+    lax.fori_loop(0, nsweep, own_band, 0, unroll=min(4, nsweep))
     for d in range(1, nt):
         for k in range(3):
             arrival(k, peer(d)).wait_recv()
@@ -148,7 +148,7 @@
         kvl[s] = total
         return total
 
-    kv_total = lax.fori_loop(0, nsweep, forward, jnp.zeros((width, width), F32), unroll=2)
+    kv_total = lax.fori_loop(0, nsweep, forward, jnp.zeros((width, width), F32), unroll=min(4, nsweep))
 
     def tile_copy(k, to, slot, sem):
         return pltpu.make_async_remote_copy(
@@ -214,7 +214,7 @@
         cotl[s] = total
         return total
 
-    cot_total = lax.fori_loop(0, nsweep, cot_sum, jnp.zeros((width, width), F32), unroll=2)
+    cot_total = lax.fori_loop(0, nsweep, cot_sum, jnp.zeros((width, width), F32), unroll=min(4, nsweep))
     send_tile(1, cot_total)
     before = take_block(0, kv_inside)
 
@@ -238,7 +238,7 @@
         return c
 
     cot_inside = send_block(1)
-    lax.fori_loop(0, nsweep, attend, 0, unroll=2)
+    lax.fori_loop(0, nsweep, attend, 0, unroll=min(4, nsweep))
     after = take_block(1, cot_inside)
 
     def backward(s, c):
@@ -255,7 +255,7 @@
         cacc[...] += mm(x3[s, W:W + cells, :], g3[slot], 0, 0)
         return c
 
-    lax.fori_loop(0, nsweep, backward, 0, unroll=2)
+    lax.fori_loop(0, nsweep, backward, 0, unroll=min(4, nsweep))
 
     nconv = 9 * width
     for a in range(3):
@@ -300,8 +300,8 @@
     each(lambda p: sum_copy(p, me).start())
     each(lambda p: sum_copy(p, p).wait_recv())
     flat = gall[...].reshape(gflat.shape)
-    gconv[...] = flat[0:nconv].astype(F32)
-    gproj[...] = flat[nconv:12 * width].astype(F32)
+    gconv[...] = flat[0:nconv]
+    gproj[...] = flat[nconv:12 * width]
 
     def drain(s, c):
         for d in range(1, nt):
@@ -342,8 +342,8 @@
         functools.partial(body, nm, nt, nsweep, per_tile, band),
         out_shape=(
             jax.ShapeDtypeStruct((block, band, width), BF),
-            jax.ShapeDtypeStruct((9 * width, width), F32),
-            jax.ShapeDtypeStruct((3 * width, width), F32),
+            jax.ShapeDtypeStruct((9 * width, width), BF),
+            jax.ShapeDtypeStruct((3 * width, width), BF),
         ),
         in_specs=[hspec] * 7,
         out_specs=(aspec, vspec, vspec),
@@ -394,8 +394,8 @@
     )
     return (
         out[0],
-        out[1].reshape(9, width, width),
-        out[2].reshape(3, 1, width, width),
+        out[1].reshape(9, width, width).astype(F32),
+        out[2].reshape(3, 1, width, width).astype(F32),
     )
 
 

time: 58.9 us -> 58.2 us (0.988)
  other arithmetic: 0 us -> 3.48 us
  local copies, waits for them, and re-layouts: 3.93 us -> 0.88 us
  Pallas kernels: 54.1 us -> 53 us
    unnamed x7 -> x3, local copies, waits for them, and re-layouts: 3.93 us -> 0.88 us
    convert_element_type x0 -> x1, other arithmetic: none -> 1.82 us  [local(): out[1].reshape(9, width, width).astype(F32)]
    unnamed x0 -> x1, other arithmetic: none -> 1.66 us
    pallas_call x1, Pallas kernels: 54.1 us -> 53 us  [local(): pl.pallas_call(functools.partial(body, nm, nt, nsweep, per_tile, band), o...]
where the time goes in v5:
time: 58.2 us; the launch traced here: 58 us
  Pallas kernels  53 us (91%)
  other arithmetic  3.48 us (6%)
  local copies, waits for them, and re-layouts  0.88 us (2%)
  between operations  0.65 us (1%)
    pallas_call x1, Pallas kernels, local(): pl.pallas_call(functools.partial(body, nm, nt, nsweep, per_tile, band), o...  53 us
    convert_element_type x1, other arithmetic, local(): out[1].reshape(9, width, width).astype(F32)  1.82 us
    unnamed x1, other arithmetic  1.66 us

profile of v5, /device:TPU:0, one launch (start us, length us, event | category | flops | bytes accessed | tf_op | source)
XLA Modules:
  0.0 58.0 jit_solution(15550119040032494339)
XLA Ops:
  0.6 53.0 %shard_map.94 = (bf16[16,192,128]{2,1,0:T(8,128)(2,1)}, bf16[1152,128]{1,0:T(8,128)(2,1)}, bf16[384,128]{1,0:T(8,128)(2,1)}) custom-call(bf16[16,96,128]{2,1,0:T(8,128)(2,1)} %feat.1, s32[2,8,96]{2,1,0:T(8,128)} %bitcast.13, s32[2,8,96]{2,1,0:T(8,128)} %bitcast.14, bf16[16,128]{1,0:T(8,128)(2,1)} %embed_in.1, bf16[3,384,128]{2,1,0:T(8,128)(2,1)} %bitcast.12, ...), custom_call_target="tpu_custom_call" | custom-call | flops 3623878656 | bytes 4194304 | tf_op jit(solution)/shard_map/pallas_call | solution.py:341
  53.6 0.0 copy-start
  53.6 1.7 %convert.4 = f32[3,1,128,128]{3,2,1,0:T(8,128)} convert(bf16[3,1,128,128]{3,2,1,0:T(8,128)(2,1)} %bitcast.11) | non-fusion elementwise | flops 49152 | bytes 294912
  55.3 1.8 %convert.2 = f32[9,128,128]{2,1,0:T(8,128)} convert(bf16[9,128,128]{2,1,0:T(8,128)(2,1)} %bitcast.10) | non-fusion elementwise | flops 147456 | bytes 884736 | tf_op jit(solution)/shard_map/convert_element_type | solution.py:397
  57.1 0.0 copy-done
  57.1 0.9 %copy.12 = bf16[16,192,128]{2,1,0:T(8,128)(2,1)} copy(bf16[16,192,128]{2,1,0:T(8,128)(2,1)S(1)} %copy-done) | data formatting | bytes 1572864
Async XLA Ops:
  53.6 3.5 %copy-start = (bf16[16,192,128]{2,1,0:T(8,128)(2,1)S(1)}, bf16[16,192,128]{2,1,0:T(8,128)(2,1)}, u32[]{:S(2)}) copy-start(bf16[16,192,128]{2,1,0:T(8,128)(2,1)} %get-tuple-element.15) | copy-start | bytes 2359300
